TPU v7x, 512 devices: a whole 4x4x16 slice. The times are simulated.
512 devices in a mesh: wide: 64 (over z, y), clus: 8 (over x, core).
Axes of the slice: x: 4, y: 4, z: 16, core: 2. Of those that a mesh axis runs over, the one named last changes fastest.
Arguments:
- duals: bfloat16 [96, 1024, 3840], P(None, ('wide', 'clus')), may hold values from -6 to 6
- kernel: bfloat16 [1024, 6, 3840], P(('wide', 'clus')), may hold values from -0.29882812 to 0.29882812
- sub_counts: int32 [512], P(('wide', 'clus')), may hold values from 1 to 2, as said below
- dual_sizes: int32 [1024], P(('wide', 'clus')), may hold values from 1920 to 3840, as said below
- cluster_factor: float32 [64, 96, 96], P('wide'), as said below
- coarse_map: int32 [64, 96], P('wide'), may hold values from 0 to 1535, as said below
- coarse_inverse: float32 [1536, 1536], P(None, 'clus'), as said below
Outputs:
- projected: bfloat16 [96, 1024, 3840], P(None, ('wide', 'clus'))
Inputs may be any that keep to these rules, and one draw needn't show every extreme that they name: `sub_counts`: each device holds 1 to 2 subdomains; some device holds 2. `dual_sizes`: some slot has the full 3840. `coarse_map`: the rows of cluster w map into the 48 global rows that begin at w * 24, counted modulo 1536. `cluster_factor`: lower triangular with diagonal entries between 1 and 2. `coarse_inverse`: diagonal entries between 1 and 2.
All inputs are finite; a program needn't handle non-finite values.
Results may differ from a plain program's by a relative error of at most 0.0018.
Values sent between devices are 32-bit elements; how exact they have to be, the bound alone decides.
A program may use at most 64 MiB of HBM per device.

v0:
```python
import jax
import jax.numpy as jnp
from jax import lax
from jax.sharding import PartitionSpec as P


def per_device(duals, kernel, sub_counts, dual_sizes, cluster_factor, coarse_map, coarse_inverse):
    rhs_count, sub_count, dual_width = duals.shape
    mode_count = kernel.shape[1]
    hi = lax.Precision.HIGHEST
    position = lax.broadcasted_iota(jnp.int32, (sub_count, dual_width), 1)
    slot_index = lax.broadcasted_iota(jnp.int32, (sub_count, dual_width), 0)
    active = (position < dual_sizes[:, None]) & (slot_index < sub_counts[0])
    masked = jnp.where(active[:, None, :], kernel, jnp.zeros_like(kernel))
    local = jnp.einsum("rsi,ski->rsk", duals, masked, preferred_element_type=jnp.float32)
    local = local.reshape(rhs_count, sub_count * mode_count)
    cluster_vec = lax.all_gather(local, "clus", axis=1, tiled=True)
    lower = cluster_factor[0]
    rows_map = coarse_map[0]
    cluster_rows = rows_map.shape[0]
    global_rows = coarse_inverse.shape[0]
    forward = lax.linalg.triangular_solve(lower, cluster_vec.T, left_side=True, lower=True).T
    one_hot = (
        rows_map[:, None] == lax.broadcasted_iota(jnp.int32, (cluster_rows, global_rows), 1)
    ).astype(jnp.float32)
    part_sum = jnp.dot(forward, one_hot, precision=hi)
    gsum = lax.psum(part_sum, "wide")
    beta_part = jnp.dot(gsum, coarse_inverse, precision=hi)
    beta = lax.all_gather(beta_part, "clus", axis=1, tiled=True)
    back = jnp.dot(beta, one_hot.T, precision=hi)
    corr = lax.linalg.triangular_solve(
        lower, (forward - back).T, left_side=True, lower=True, transpose_a=True
    )
    own_rows = lax.dynamic_slice_in_dim(
        corr, lax.axis_index("clus") * sub_count * mode_count, sub_count * mode_count, 0
    )
    own_corr = own_rows.T.reshape(rhs_count, sub_count, mode_count).astype(jnp.bfloat16)
    delta = jnp.einsum("rsk,ski->rsi", own_corr, masked, preferred_element_type=jnp.float32)
    return (duals.astype(jnp.float32) - delta).astype(jnp.bfloat16)


def solution(mesh):
    in_specs = (
        P(None, ("wide", "clus"), None),
        P(("wide", "clus"), None, None),
        P(("wide", "clus")),
        P(("wide", "clus")),
        P("wide", None, None),
        P("wide", None),
        P(None, "clus"),
    )
    out_specs = P(None, ("wide", "clus"), None)
    return jax.shard_map(
        per_device, mesh=mesh, in_specs=in_specs, out_specs=out_specs, check_vma=False
    )
```

profile of v0, /device:TPU:1, one launch (start us, length us, event | category | flops | bytes accessed | tf_op | source)
XLA Modules:
  0.0 332.0 jit_solution(3179815879013616364)
XLA Ops:
  6.5 0.0 copy-start
  6.5 0.0 copy-start.2
  6.5 0.0 all-reduce.2.cloned.1.call-start
  7.3 0.8 fusion.16
  8.1 7.4 %custom-call.5 = f32[1,96,96]{1,2,0:T(8,128)S(1)} custom-call(f32[1,96,96]{2,1,0:T(8,128)S(1)} %fusion.16), custom_call_target="InvertDiagBlocksLowerTriangular" | custom-call | tf_op jit(solution)/shard_map/triangular_solve | solution.py:31
  15.5 0.7 compare_and_fusion
  16.2 1.0 broadcast_select_fusion
  17.2 1.9 fusion.4
  19.1 19.4 %all-gather = f32[8,12,96]{2,1,0:T(8,128)S(1)} all-gather(f32[1,12,96]{2,1,0:T(8,128)S(1)} %bitcast.34), channel_id=1, replica_groups=mesh['wide'=64,'clus'=8] {'clus'}, dimensions={0}, use_global_device_ids=true | all-gather | bytes 41472 | tf_op jit(solution)/shard_map/all_gather | solution.py:17
  38.5 0.3 fusion.14
  38.8 0.0 copy-done.2
  38.8 1.3 fusion.7
  40.1 0.0 all-reduce.2.cloned.1.call-update
  40.1 0.0 copy-start.1
  40.1 254.5 %all-reduce.2.cloned.1.call-done = f32[96,1536]{1,0:T(8,128)} async-done(((f32[96,1536]{1,0:T(8,128)}), f32[96,1536]{1,0:T(8,128)}) %all-reduce.2.cloned.1.call-update) | async-done | bytes 589840 | tf_op jit(solution)/shard_map/psum | solution.py:27
  294.6 0.0 copy-done
  294.6 2.1 fusion.18
  296.8 24.4 %all_gather.7 = f32[96,1536]{0,1:T(8,128)S(1)} all-gather(f32[96,192]{0,1:T(8,128)S(1)} %fusion.18), channel_id=1, replica_groups=mesh['wide'=64,'clus'=8] {'clus'}, dimensions={1}, use_global_device_ids=true | all-gather | bytes 663552 | tf_op jit(solution)/shard_map/all_gather | solution.py:29
  321.1 0.5 convolution_subtract_fusion
  321.7 0.2 fusion.12
  321.9 0.0 copy-done.1
  321.9 0.6 fusion.1
  322.5 2.6 copy.24
  (5 shorter events, 0.1 us)
Async XLA Ops:
  6.5 288.1 %copy-start = (f32[1536,192]{0,1:T(8,128)S(1)}, f32[1536,192]{0,1:T(8,128)}, u32[]{:S(2)}) copy-start(f32[1536,192]{0,1:T(8,128)} %param.13) | copy-start | bytes 3538948
  6.5 32.3 %copy-start.2 = (s32[1,96]{1,0:T(1,128)S(1)}, s32[1,96]{1,0:T(1,128)}, u32[]{:S(2)}) copy-start(s32[1,96]{1,0:T(1,128)} %param.12) | copy-start | bytes 1156
  6.5 288.1 %all-reduce.2.cloned.1.call-start = ((), (), s32[]{:S(2)}) async-start(), calls=%async_computation | async-start | bytes 1179648 | tf_op jit(solution)/shard_map/psum | solution.py:27
  40.1 281.8 %copy-start.1 = (bf16[96,2,3840]{2,1,0:T(2,128)(2,1)S(1)}, bf16[96,2,3840]{2,1,0:T(2,128)(2,1)}, u32[]{:S(2)}) copy-start(bf16[96,2,3840]{2,1,0:T(2,128)(2,1)} %param.7) | copy-start | bytes 4423684
Sparse Core Ops, SparseCore 0:
  40.2 254.3 all-reduce.1
where the time goes:
time: 332 us
  waiting for transfers between devices  254 us (77%)
  blocking collectives  43.8 us (13%)
  between operations  14.2 us (4%)
  other arithmetic  9.9 us (3%)
  matrix products  6.85 us (2%)
    psum x1, waiting for transfers between devices, per_device(): gsum = lax.psum(part_sum, 'wide')  254 us
    all_gather x1, blocking collectives, per_device(): beta = lax.all_gather(beta_part, 'clus', axis=1, tiled=True)  24.4 us
    all_gather x1, blocking collectives, per_device(): cluster_vec = lax.all_gather(local, 'clus', axis=1, tiled=True)  19.4 us
    another operation x2, other arithmetic, per_device(): lax.linalg.triangular_solve(lower, (forward - back).T, left_side=True, lo...  8.16 us
  transfers between devices with their start and end apart: 1, of which 1 were waited for; matrix products, arithmetic and copies ran while one was open for 0% of the time, Pallas kernels for 0%

commit v1 on v0

v1 whole, which is shorter than its diff:
```python
import functools

import jax
import jax.numpy as jnp
from jax import lax
from jax.experimental import pallas as pl
from jax.experimental.pallas import tpu as pltpu
from jax.sharding import PartitionSpec as P

MESH = pl.DeviceIdType.MESH
NZ, NY, NT = 16, 4, 8
NW = NZ * NY
BAND = 24
GK = NW * BAND
CK = 96
RHS = 96
LANES = 128


def mm(a, b, dims=((1,), (0,))):
    return lax.dot_general(
        a, b, (dims, ((), ())), precision=lax.Precision.HIGHEST, preferred_element_type=jnp.float32
    )


def lower_inverse(lower):
    n = lower.shape[0]
    blocks = n // 8
    l3 = lower.reshape(blocks, 8, n)
    bi = lax.broadcasted_iota(jnp.int32, (blocks, 8, n), 0)
    ri = lax.broadcasted_iota(jnp.int32, (blocks, 8, n), 1)
    ci = lax.broadcasted_iota(jnp.int32, (blocks, 8, n), 2)
    own = ci - 8 * bi
    x = jnp.where(own == ri, 1.0, 0.0)
    rdiag = 1.0 / jnp.sum(jnp.where(own == ri, l3, 0.0), axis=2, keepdims=True)
    row = lax.broadcasted_iota(jnp.int32, (blocks, 8, 1), 1)
    for j in range(8):
        col = jnp.sum(jnp.where(own == j, l3, 0.0), axis=2, keepdims=True)
        pivot = x[:, j : j + 1, :] * rdiag[:, j : j + 1, :]
        x = jnp.where(row == j, pivot, x - jnp.where(row > j, col, 0.0) * pivot)
    x = x.reshape(n, n)
    r2 = lax.broadcasted_iota(jnp.int32, (n, n), 0)
    c2 = lax.broadcasted_iota(jnp.int32, (n, n), 1)
    size = 8
    while size < n:
        pair = 2 * size
        off = (r2 // pair == c2 // pair) & (r2 % pair >= size) & (c2 % pair < size)
        x = x - mm(x, mm(jnp.where(off, lower, 0.0), x))
        size = pair
    return x


def coarse_kernel(
    yl, low, cmap, ct, out,
    ysend, yall, gsec, gprev, cst, cpk, c48, gbuf, part, crecv,
    lsem, y_s, y_r, g_s, g_r, c_s, c_r, z_s, z_r, v_s, v_r, d_s, d_r,
):
    w = lax.axis_index("wide")
    t = lax.axis_index("clus")
    z, y = w // NY, w % NY
    wn, wp = (w + 1) % NW, (w + NW - 1) % NW
    root_n = (wn // NY) % NT
    is_root = t == z % NT
    zh = z // NT
    cs0, cs1 = w // NT, wn // NT

    def at(ww, tt):
        return (ww, tt)

    def zdev(zz):
        return (zz * NY + y, t)

    @pl.when(t == cs0)
    def _():
        pltpu.make_async_copy(
            ct.at[pl.ds(pl.multiple_of((w % NT) * BAND, 8), BAND)], cst.at[0], lsem.at[0]
        ).start()

    @pl.when(t == cs1)
    def _():
        pltpu.make_async_copy(
            ct.at[pl.ds(pl.multiple_of((wn % NT) * BAND, 8), BAND)], cst.at[1], lsem.at[1]
        ).start()

    gbuf[...] = jnp.zeros_like(gbuf)
    barrier = pltpu.get_barrier_semaphore()

    def greet(dev):
        pl.semaphore_signal(barrier, inc=1, device_id=dev, device_id_type=MESH)

    for k in range(1, NT):
        greet(at(w, (t + k) % NT))
    for k in range(1, NY):
        greet((z * NY + (y + k) % NY, t))
    greet(at(wn, root_n))
    for zz in (t, t + NT):
        @pl.when(zz != z)
        def _():
            greet(zdev(zz))

    @pl.when(is_root)
    def _():
        for k in range(NT):
            greet(at(wp, k))
        for k in range(1, NZ):
            greet(zdev((z + k) % NZ))

    ysend[...] = jnp.zeros_like(ysend)
    ysend[0:6, 0:RHS] = yl[0]
    ysend[8:14, 0:RHS] = yl[1]

    pl.semaphore_wait(barrier, jnp.where(is_root, 35, 13))

    to_next = pltpu.make_async_remote_copy(
        ysend, yall.at[NT + t], y_s.at[0], y_r.at[NT + t], at(wn, root_n), MESH
    )
    to_next.start()
    to_own = pltpu.make_async_remote_copy(
        ysend, yall.at[t], y_s.at[1], y_r.at[t], at(w, z % NT), MESH
    )

    @pl.when(jnp.logical_not(is_root))
    def _():
        to_own.start()

    @pl.when(is_root)
    def _():
        yall[t] = ysend[...]

    def cpiece(half, tt, k):
        return pltpu.make_async_remote_copy(
            cpk.at[half, tt],
            c48.at[half],
            c_s.at[half, k],
            c_r.at[half],
            at(w, tt),
            MESH,
        )

    for half, src in ((0, cs0), (1, cs1)):
        @pl.when(t == src)
        def _():
            pltpu.make_async_copy(ct.at[pl.ds(0, BAND)], cst.at[half], lsem.at[half]).wait()
            for zz in range(NZ):
                cpk[half, zz % NT, :, zz // NT * LANES : zz // NT * LANES + CK] = cst[
                    half, :, zz * CK : zz * CK + CK
                ]
            for tt in range(NT):
                for side in range(2):
                    cpk[half, tt, :, side * LANES + CK : (side + 1) * LANES] = jnp.zeros(
                        (BAND, LANES - CK), jnp.float32
                    )
            for k in range(1, NT):
                cpiece(half, (t + k) % NT, k).start()
            c48[half] = cpk[half, t]

    linv = lower_inverse(low[...])
    mi = lax.broadcasted_iota(jnp.int32, (CK, LANES), 0)
    pi = lax.broadcasted_iota(jnp.int32, (CK, LANES), 1)
    spread = jnp.where((mi == 6 * (pi // 8) + pi % 8) & (pi % 8 < 6), 1.0, 0.0)
    lpad = mm(linv, spread)
    rel = cmap[...] - w * BAND
    rel = jnp.where(rel < 0, rel + GK, rel)
    pt = jnp.where(rel == lax.broadcasted_iota(jnp.int32, (2 * BAND, CK), 0), 1.0, 0.0)
    g = mm(pt, lpad)
    gsec[...] = g[BAND:]

    send_g = pltpu.make_async_remote_copy(gsec, gprev, g_s, g_r, at(wn, root_n), MESH)

    @pl.when(t == root_n)
    def _():
        send_g.start()

    def zcopy(k):
        rows = pl.ds(pl.multiple_of(y * BAND, 8), BAND)
        return pltpu.make_async_remote_copy(
            gbuf.at[zh, rows], gbuf.at[zh, rows], z_s.at[k], z_r.at[zh], zdev((z + k) % NZ), MESH
        )

    @pl.when(is_root)
    def _():
        for k in range(2 * NT):
            @pl.when(k != t)
            def _():
                pltpu.make_async_remote_copy(
                    ysend, yall.at[k], y_s.at[1], y_r.at[k], at(w, t), MESH
                ).wait_recv()
        send_g.wait_recv()
        own = yall[0:NT].reshape(NT * 16, LANES)
        prev = yall[NT : 2 * NT].reshape(NT * 16, LANES)
        gs = mm(g[:BAND], own) + mm(gprev[...], prev)
        gbuf[zh, pl.ds(pl.multiple_of(y * BAND, 8), BAND), :] = gs
        for k in (8, 7, 9, 6, 10, 5, 11, 4, 12, 3, 13, 2, 14, 1, 15):
            zcopy(k).start()

    for half, src in ((0, cs0), (1, cs1)):
        @pl.when(t != src)
        def _():
            cpiece(half, t, 0).wait_recv()
    c2 = c48[...].reshape(2 * BAND, 2 * LANES)
    oper = mm(g, c2, ((0,), (0,)))

    def ycopy(h, k):
        rows = pl.ds(pl.multiple_of(y * BAND, 8), BAND)
        return pltpu.make_async_remote_copy(
            gbuf.at[h, rows], gbuf.at[h, rows], v_s.at[h, k], v_r.at[h, k], (z * NY + (y + k) % NY, t), MESH
        )

    def yrecv(h, k):
        rows = pl.ds(pl.multiple_of((y + NY - k) % NY * BAND, 8), BAND)
        return pltpu.make_async_remote_copy(
            gbuf.at[h, rows], gbuf.at[h, rows], v_s.at[h, k], v_r.at[h, k], (z * NY + (y + k) % NY, t), MESH
        )

    for h in range(2):
        @pl.when(jnp.logical_not(is_root & (zh == h)))
        def _():
            rows = pl.ds(pl.multiple_of(y * BAND, 8), BAND)
            pltpu.make_async_remote_copy(
                gbuf.at[h, rows], gbuf.at[h, rows], z_s.at[0], z_r.at[h], zdev((z + 1) % NZ), MESH
            ).wait_recv()
        for k in (2, 1, 3):
            ycopy(h, k).start()
    for h in range(2):
        for k in range(1, NY):
            yrecv(h, k).wait_recv()

    total = -mm(oper, gbuf[...].reshape(2 * LANES, LANES))
    part[...] = total.reshape(NT, 16, LANES)

    @pl.when(is_root)
    def _():
        own = yall[0:NT].reshape(NT * 16, LANES)
        part[...] += mm(lpad, mm(lpad, own), ((0,), (0,))).reshape(NT, 16, LANES)

    def dcopy(k):
        return pltpu.make_async_remote_copy(
            part.at[(t + k) % NT], crecv.at[k], d_s.at[k], d_r.at[k], at(w, (t + k) % NT), MESH
        )

    for k in (4, 3, 5, 2, 6, 1, 7):
        dcopy(k).start()
    acc = part[t]
    for k in range(1, NT):
        dcopy(k).wait_recv()
        acc += crecv[k]
    acc = acc.astype(out.dtype)
    out[0] = acc[0:6, 0:RHS]
    out[1] = acc[8:14, 0:RHS]

    to_next.wait_send()

    @pl.when(jnp.logical_not(is_root))
    def _():
        to_own.wait_send()

    for half, src in ((0, cs0), (1, cs1)):
        @pl.when(t == src)
        def _():
            for k in range(1, NT):
                cpiece(half, (t + k) % NT, k).wait_send()

    @pl.when(t == root_n)
    def _():
        send_g.wait_send()

    @pl.when(is_root)
    def _():
        for k in range(1, NZ):
            zcopy(k).wait_send()

    for h in range(2):
        for k in range(1, NY):
            ycopy(h, k).wait_send()
    for k in range(1, NT):
        dcopy(k).wait_send()


def coarse(yl, low, cmap, ct):
    vmem = pl.BlockSpec(memory_space=pltpu.VMEM)
    f32 = jnp.float32
    dma = pltpu.SemaphoreType.DMA
    return pl.pallas_call(
        coarse_kernel,
        out_shape=jax.ShapeDtypeStruct((2, 6, RHS), jnp.bfloat16),
        in_specs=[vmem, vmem, vmem, pl.BlockSpec(memory_space=pl.ANY)],
        out_specs=vmem,
        scratch_shapes=[
            pltpu.VMEM((16, LANES), f32),
            pltpu.VMEM((2 * NT, 16, LANES), f32),
            pltpu.VMEM((BAND, LANES), f32),
            pltpu.VMEM((BAND, LANES), f32),
            pltpu.VMEM((2, BAND, GK), f32),
            pltpu.VMEM((2, NT, BAND, 2 * LANES), f32),
            pltpu.VMEM((2, BAND, 2 * LANES), f32),
            pltpu.VMEM((2, LANES, LANES), f32),
            pltpu.VMEM((NT, 16, LANES), f32),
            pltpu.VMEM((NT, 16, LANES), f32),
            dma((2,)),
            dma((2,)), dma((2 * NT,)),
            dma, dma,
            dma((2, NT)), dma((2,)),
            dma((NZ,)), dma((2,)),
            dma((2, NY)), dma((2, NY)),
            dma((NT,)), dma((NT,)),
        ],
        compiler_params=pltpu.CompilerParams(collective_id=0, has_side_effects=True),
    )(yl, low, cmap, ct)


def per_device(duals, kernel, sub_counts, dual_sizes, cluster_factor, coarse_map, coarse_inverse):
    rhs_count, sub_count, dual_width = duals.shape
    position = lax.broadcasted_iota(jnp.int32, (sub_count, dual_width), 1)
    slot_index = lax.broadcasted_iota(jnp.int32, (sub_count, dual_width), 0)
    active = (position < dual_sizes[:, None]) & (slot_index < sub_counts[0])
    masked = jnp.where(active[:, None, :], kernel, jnp.zeros_like(kernel))
    local = jnp.einsum("rsi,ski->skr", duals, masked, preferred_element_type=jnp.float32)
    corr = coarse(local, cluster_factor[0], coarse_map, coarse_inverse.T)
    delta = jnp.einsum("skr,ski->rsi", corr, masked, preferred_element_type=jnp.float32)
    return (duals.astype(jnp.float32) - delta).astype(jnp.bfloat16)


def solution(mesh):
    in_specs = (
        P(None, ("wide", "clus"), None),
        P(("wide", "clus"), None, None),
        P(("wide", "clus")),
        P(("wide", "clus")),
        P("wide", None, None),
        P("wide", None),
        P(None, "clus"),
    )
    out_specs = P(None, ("wide", "clus"), None)
    return jax.shard_map(
        per_device, mesh=mesh, in_specs=in_specs, out_specs=out_specs, check_vma=False
    )
```

time: 332 us -> 46.5 us (0.14)
  waiting for transfers between devices: 254 us -> 0 us
  blocking collectives: 43.8 us -> 0 us
  Pallas kernels: 0 us -> 37.3 us
  between operations: 14.2 us -> 0.69 us
  other arithmetic: 9.9 us -> 1.85 us
    psum x1 -> x0, waiting for transfers between devices: 254 us -> none  [per_device(): gsum = lax.psum(part_sum, 'wide')]
    all_gather x2 -> x0, blocking collectives: 43.8 us -> none  [the longest x1 24.4 us: per_device(): beta = lax.all_gather(beta_part, 'clus', axis=1, tiled=True)]
    pallas_call x0 -> x1, Pallas kernels: none -> 37.3 us  [coarse(): pl.pallas_call(coarse_kernel, out_shape=jax.ShapeDtypeStruct((2, 6, RHS),...]
    another operation x2 -> x0, other arithmetic: 8.16 us -> none  [per_device(): lax.linalg.triangular_solve(lower, (forward - back).T, left_side=True, lo...]
  transfers between devices with their start and end apart: 1 -> 0, of which waited for: 1 -> 0; matrix products, arithmetic and copies ran while one was open for 0% -> 0% of each run, Pallas kernels for 0% -> 0%
where the time goes in v1:
time: 46.5 us; the launch traced here: 46.2 us
  Pallas kernels  37.3 us (80%)
  matrix products  3.72 us (8%)
  local copies, waits for them, and re-layouts  2.63 us (6%)
  other arithmetic  1.85 us (4%)
  between operations  0.69 us (1%)
    pallas_call x1, Pallas kernels, coarse(): pl.pallas_call(coarse_kernel, out_shape=jax.ShapeDtypeStruct((2, 6, RHS),...  37.3 us
    convert_element_type x1, local copies, waits for them, and re-layouts, per_device(): return (duals.astype(jnp.float32) - delta).astype(jnp.bfloat16)  2.63 us
    dot_general x1, matrix products, per_device(): jnp.einsum('rsi,ski->skr', duals, masked, preferred_element_type=jnp.floa...  2.47 us
    dot_general x1, matrix products, per_device(): jnp.einsum('skr,ski->rsi', corr, masked, preferred_element_type=jnp.float32)  1.25 us
    select_n x1, other arithmetic, per_device(): masked = jnp.where(active[:, None, :], kernel, jnp.zeros_like(kernel))  1.09 us

profile of v1, /device:TPU:1, one launch (start us, length us, event | category | flops | bytes accessed | tf_op | source)
XLA Modules:
  0.0 46.2 jit_solution(16289750335349016094)
XLA Ops:
  0.7 0.7 %compare_and_fusion = pred[2,3840]{1,0:T(4,128)(4,1)S(1)} fusion(pred[2]{0:T(512)(128)(4,1)S(1)} %iota_compare_fusion, s32[2]{0:T(128)} %param.10), kind=kLoop, calls=%fused_computation.8 | loop fusion | flops 15360 | bytes 7690 | tf_op jit(solution)/shard_map/and | solution.py:315
  1.4 0.0 copy-start
  1.4 1.1 %broadcast_select_fusion = bf16[2,6,3840]{2,0,1:T(2,128)(2,1)S(1)} fusion(bf16[2,6,3840]{2,0,1:T(2,128)(2,1)} %param.8, pred[2,3840]{1,0:T(4,128)(4,1)S(1)} %compare_and_fusion), kind=kLoop, calls=%fused_computation.5 | loop fusion | flops 46080 | bytes 192000 | tf_op jit(solution)/shard_map/jit(_where)/select_n | solution.py:316
  2.5 2.5 %fusion.2.yl = f32[2,6,96]{2,1,0:T(8,128)} fusion(bf16[96,2,3840]{2,1,0:T(2,128)(2,1)} %param.7, bf16[2,6,3840]{2,0,1:T(2,128)(2,1)S(1)} %broadcast_select_fusion), kind=kOutput, calls=%fused_computation.3 | convolution fusion | flops 8847360 | bytes 1571328 | tf_op jit(solution)/shard_map/rsi,ski->skr/dot_general | solution.py:317
  5.0 37.3 %shard_map.73 = bf16[2,6,96]{2,1,0:T(8,128)(2,1)} custom-call(f32[2,6,96]{2,1,0:T(8,128)} %fusion.2.yl, f32[96,96]{1,0:T(8,128)} %bitcast.12, s32[1,96]{1,0:T(1,128)} %cmap.1, f32[192,1536]{1,0:T(8,128)} %bitcast.11), custom_call_target="tpu_custom_call" | custom-call | tf_op jit(solution)/shard_map/pallas_call | solution.py:283
  42.3 0.0 copy-done
  42.3 1.3 %fusion.1 = bf16[96,2,3840]{2,0,1:T(8,128)(2,1)S(1)} fusion(bf16[2,6,96]{2,1,0:T(8,128)(2,1)} %shard_map.73, bf16[96,2,3840]{2,1,0:T(2,128)(2,1)S(1)} %copy-done, bf16[2,6,3840]{2,0,1:T(2,128)(2,1)S(1)} %broadcast_select_fusion), kind=kOutput, calls=%fused_computation.2 | convolution fusion | flops 11059200 | bytes 3043584 | tf_op jit(solution)/shard_map/skr,ski->rsi/dot_general | solution.py:319
  43.6 2.6 %copy.10 = bf16[96,2,3840]{2,1,0:T(2,128)(2,1)} copy(bf16[96,2,3840]{2,0,1:T(8,128)(2,1)S(1)} %fusion.1) | data formatting | bytes 2949120 | tf_op jit(solution)/shard_map/convert_element_type | solution.py:320
  (1 shorter events, 0.0 us)
Async XLA Ops:
  1.4 40.9 %copy-start = (bf16[96,2,3840]{2,1,0:T(2,128)(2,1)S(1)}, bf16[96,2,3840]{2,1,0:T(2,128)(2,1)}, u32[]{:S(2)}) copy-start(bf16[96,2,3840]{2,1,0:T(2,128)(2,1)} %param.7) | copy-start | bytes 4423684

commit v2 on v1

--- a/solution.py
+++ b/solution.py
@@ -50,10 +50,19 @@
     return x
 
 
+def masked_rows(kern, count, size0, size1):
+    rows = kern.reshape(12, kern.shape[-1])
+    slot = lax.broadcasted_iota(jnp.int32, rows.shape, 0) % 2
+    pos = lax.broadcasted_iota(jnp.int32, rows.shape, 1)
+    limit = jnp.where(slot == 0, jnp.where(count > 0, size0, 0), jnp.where(count > 1, size1, 0))
+    return jnp.where(pos < limit, rows.astype(jnp.float32), 0.0).astype(jnp.bfloat16)
+
+
 def coarse_kernel(
-    yl, low, cmap, ct, out,
+    duals, kern, counts, sizes, low_in, cmap_in, ct, out,
+    dbuf, kbuf, nbuf, sbuf, low, cmap,
     ysend, yall, gsec, gprev, cst, cpk, c48, gbuf, part, crecv,
-    lsem, y_s, y_r, g_s, g_r, c_s, c_r, z_s, z_r, v_s, v_r, d_s, d_r,
+    isem, lsem, y_s, y_r, g_s, g_r, c_s, c_r, z_s, z_r, v_s, v_r, d_s, d_r,
 ):
     w = lax.axis_index("wide")
     t = lax.axis_index("clus")
@@ -70,54 +79,68 @@
     def zdev(zz):
         return (zz * NY + y, t)
 
-    @pl.when(t == cs0)
-    def _():
-        pltpu.make_async_copy(
-            ct.at[pl.ds(pl.multiple_of((w % NT) * BAND, 8), BAND)], cst.at[0], lsem.at[0]
-        ).start()
-
-    @pl.when(t == cs1)
-    def _():
-        pltpu.make_async_copy(
-            ct.at[pl.ds(pl.multiple_of((wn % NT) * BAND, 8), BAND)], cst.at[1], lsem.at[1]
-        ).start()
-
     gbuf[...] = jnp.zeros_like(gbuf)
+
     barrier = pltpu.get_barrier_semaphore()
 
     def greet(dev):
         pl.semaphore_signal(barrier, inc=1, device_id=dev, device_id_type=MESH)
+
+    for zz in (t, t + NT):
+        @pl.when(zz != z)
+        def _():
+            greet(zdev(zz))
 
     for k in range(1, NT):
         greet(at(w, (t + k) % NT))
     for k in range(1, NY):
         greet((z * NY + (y + k) % NY, t))
-    greet(at(wn, root_n))
-    for zz in (t, t + NT):
-        @pl.when(zz != z)
-        def _():
-            greet(zdev(zz))
 
     @pl.when(is_root)
     def _():
         for k in range(NT):
             greet(at(wp, k))
-        for k in range(1, NZ):
-            greet(zdev((z + k) % NZ))
+
+    loads = [
+        pltpu.make_async_copy(src, dst, isem.at[i])
+        for i, (src, dst) in enumerate(
+            ((kern, kbuf), (counts, nbuf), (sizes, sbuf), (duals, dbuf), (low_in, low), (cmap_in, cmap))
+        )
+    ]
+    for load in loads:
+        load.start()
+
+    @pl.when(t == cs0)
+    def _():
+        pltpu.make_async_copy(
+            ct.at[pl.ds(pl.multiple_of((w % NT) * BAND, 8), BAND)], cst.at[0], lsem.at[0]
+        ).start()
+
+    @pl.when(t == cs1)
+    def _():
+        pltpu.make_async_copy(
+            ct.at[pl.ds(pl.multiple_of((wn % NT) * BAND, 8), BAND)], cst.at[1], lsem.at[1]
+        ).start()
 
     ysend[...] = jnp.zeros_like(ysend)
-    ysend[0:6, 0:RHS] = yl[0]
-    ysend[8:14, 0:RHS] = yl[1]
-
-    pl.semaphore_wait(barrier, jnp.where(is_root, 35, 13))
+    for load in loads[:4]:
+        load.wait()
+    masked = masked_rows(kbuf[...], nbuf[0], sbuf[0], sbuf[1]).reshape(6, 2, -1)
+    local = lax.dot_general(
+        masked, dbuf[...], (((2,), (2,)), ((1,), (1,))), preferred_element_type=jnp.float32
+    )
+    for slot in range(2):
+        ysend[pl.ds(slot, 6, stride=2), 0:RHS] = local[slot]
+
+    pl.semaphore_wait(barrier, jnp.where(is_root, 26, 11))
 
     to_next = pltpu.make_async_remote_copy(
         ysend, yall.at[NT + t], y_s.at[0], y_r.at[NT + t], at(wn, root_n), MESH
     )
-    to_next.start()
     to_own = pltpu.make_async_remote_copy(
         ysend, yall.at[t], y_s.at[1], y_r.at[t], at(w, z % NT), MESH
     )
+    to_next.start()
 
     @pl.when(jnp.logical_not(is_root))
     def _():
@@ -154,10 +177,15 @@
                 cpiece(half, (t + k) % NT, k).start()
             c48[half] = cpk[half, t]
 
+    for load in loads[4:]:
+        load.wait()
     linv = lower_inverse(low[...])
     mi = lax.broadcasted_iota(jnp.int32, (CK, LANES), 0)
     pi = lax.broadcasted_iota(jnp.int32, (CK, LANES), 1)
-    spread = jnp.where((mi == 6 * (pi // 8) + pi % 8) & (pi % 8 < 6), 1.0, 0.0)
+    slot_row = pi % 16
+    spread = jnp.where(
+        (mi == 12 * (pi // 16) + 6 * (slot_row % 2) + slot_row // 2) & (slot_row < 12), 1.0, 0.0
+    )
     lpad = mm(linv, spread)
     rel = cmap[...] - w * BAND
     rel = jnp.where(rel < 0, rel + GK, rel)
@@ -244,9 +272,7 @@
     for k in range(1, NT):
         dcopy(k).wait_recv()
         acc += crecv[k]
-    acc = acc.astype(out.dtype)
-    out[0] = acc[0:6, 0:RHS]
-    out[1] = acc[8:14, 0:RHS]
+    out[...] = acc.astype(out.dtype)
 
     to_next.wait_send()
 
@@ -276,16 +302,22 @@
         dcopy(k).wait_send()
 
 
-def coarse(yl, low, cmap, ct):
-    vmem = pl.BlockSpec(memory_space=pltpu.VMEM)
+def coarse(duals, kern, counts, sizes, low, cmap, ct):
+    hbm = pl.BlockSpec(memory_space=pl.ANY)
     f32 = jnp.float32
     dma = pltpu.SemaphoreType.DMA
     return pl.pallas_call(
         coarse_kernel,
-        out_shape=jax.ShapeDtypeStruct((2, 6, RHS), jnp.bfloat16),
-        in_specs=[vmem, vmem, vmem, pl.BlockSpec(memory_space=pl.ANY)],
-        out_specs=vmem,
+        out_shape=jax.ShapeDtypeStruct((16, LANES), jnp.bfloat16),
+        in_specs=[hbm] * 7,
+        out_specs=pl.BlockSpec(memory_space=pltpu.VMEM),
         scratch_shapes=[
+            pltpu.VMEM(duals.shape, duals.dtype),
+            pltpu.VMEM(kern.shape, kern.dtype),
+            pltpu.SMEM(counts.shape, jnp.int32),
+            pltpu.SMEM(sizes.shape, jnp.int32),
+            pltpu.VMEM(low.shape, f32),
+            pltpu.VMEM(cmap.shape, jnp.int32),
             pltpu.VMEM((16, LANES), f32),
             pltpu.VMEM((2 * NT, 16, LANES), f32),
             pltpu.VMEM((BAND, LANES), f32),
@@ -296,6 +328,7 @@
             pltpu.VMEM((2, LANES, LANES), f32),
             pltpu.VMEM((NT, 16, LANES), f32),
             pltpu.VMEM((NT, 16, LANES), f32),
+            dma((6,)),
             dma((2,)),
             dma((2,)), dma((2 * NT,)),
             dma, dma,
@@ -305,19 +338,66 @@
             dma((NT,)), dma((NT,)),
         ],
         compiler_params=pltpu.CompilerParams(collective_id=0, has_side_effects=True),
-    )(yl, low, cmap, ct)
+    )(duals, kern, counts, sizes, low, cmap, ct)
+
+
+PIECES = 6
+
+
+def project_kernel(duals, kern, counts, sizes, corr, out, obuf, sem):
+    masked = masked_rows(kern[...], counts[0], sizes[0], sizes[1])
+    rows = 2 * RHS
+    pick = jnp.where(
+        lax.broadcasted_iota(jnp.int32, (rows, LANES), 0) // 2
+        == lax.broadcasted_iota(jnp.int32, (rows, LANES), 1),
+        1.0,
+        0.0,
+    ).astype(jnp.bfloat16)
+    wide = lax.dot_general(
+        pick, corr[...], (((1,), (1,)), ((), ())), preferred_element_type=jnp.float32
+    )
+    same = (
+        lax.broadcasted_iota(jnp.int32, wide.shape, 0) % 2
+        == lax.broadcasted_iota(jnp.int32, wide.shape, 1) % 2
+    )
+    wide = jnp.where(same, wide, 0.0).astype(jnp.bfloat16)[:, :12]
+    step = RHS // PIECES
+    copies = []
+    for i in range(PIECES):
+        part = pl.ds(i * step, step)
+        block = duals[part].reshape(2 * step, -1).astype(jnp.float32)
+        delta = jnp.dot(
+            wide[2 * step * i : 2 * step * (i + 1)], masked, preferred_element_type=jnp.float32
+        )
+        obuf[part] = (block - delta).astype(out.dtype).reshape(step, 2, -1)
+        copy = pltpu.make_async_copy(obuf.at[part], out.at[part], sem.at[i])
+        copy.start()
+        copies.append(copy)
+    for copy in copies:
+        copy.wait()
+
+
+def project(duals, kern, counts, sizes, corr):
+    vmem = pl.BlockSpec(memory_space=pltpu.VMEM)
+    smem = pl.BlockSpec(memory_space=pltpu.SMEM)
+    return pl.pallas_call(
+        project_kernel,
+        out_shape=jax.ShapeDtypeStruct(duals.shape, duals.dtype),
+        in_specs=[vmem, vmem, smem, smem, vmem],
+        out_specs=pl.BlockSpec(memory_space=pl.ANY),
+        scratch_shapes=[
+            pltpu.VMEM(duals.shape, duals.dtype),
+            pltpu.SemaphoreType.DMA((PIECES,)),
+        ],
+    )(duals, kern, counts, sizes, corr)
 
 
 def per_device(duals, kernel, sub_counts, dual_sizes, cluster_factor, coarse_map, coarse_inverse):
-    rhs_count, sub_count, dual_width = duals.shape
-    position = lax.broadcasted_iota(jnp.int32, (sub_count, dual_width), 1)
-    slot_index = lax.broadcasted_iota(jnp.int32, (sub_count, dual_width), 0)
-    active = (position < dual_sizes[:, None]) & (slot_index < sub_counts[0])
-    masked = jnp.where(active[:, None, :], kernel, jnp.zeros_like(kernel))
-    local = jnp.einsum("rsi,ski->skr", duals, masked, preferred_element_type=jnp.float32)
-    corr = coarse(local, cluster_factor[0], coarse_map, coarse_inverse.T)
-    delta = jnp.einsum("skr,ski->rsi", corr, masked, preferred_element_type=jnp.float32)
-    return (duals.astype(jnp.float32) - delta).astype(jnp.bfloat16)
+    kern = kernel.transpose(1, 0, 2)
+    corr = coarse(
+        duals, kern, sub_counts, dual_sizes, cluster_factor[0], coarse_map, coarse_inverse.T
+    )
+    return project(duals, kern, sub_counts, dual_sizes, corr)
 
 
 def solution(mesh):

time: 46.5 us -> 40.7 us (0.88)
  matrix products: 3.72 us -> 0 us
  local copies, waits for them, and re-layouts: 2.63 us -> 0 us
  Pallas kernels: 37.3 us -> 39.9 us
  other arithmetic: 1.85 us -> 0 us
    dot_general x2 -> x0, matrix products: 3.72 us -> none  [the longest x1 2.47 us: per_device(): jnp.einsum('rsi,ski->skr', duals, masked, preferred_element_type=jnp.floa...]
    convert_element_type x1 -> x0, local copies, waits for them, and re-layouts: 2.63 us -> none  [per_device(): return (duals.astype(jnp.float32) - delta).astype(jnp.bfloat16)]
    pallas_call x1 -> x2, Pallas kernels: 37.3 us -> 39.9 us  [the longest x1 36.4 us: coarse(): pl.pallas_call(coarse_kernel, out_shape=jax.ShapeDtypeStruct((16, LANES),...]
    select_n x1 -> x0, other arithmetic: 1.09 us -> none  [per_device(): masked = jnp.where(active[:, None, :], kernel, jnp.zeros_like(kernel))]
    and x1 -> x0, other arithmetic: 0.75 us -> none  [per_device(): active = (position < dual_sizes[:, None]) & (slot_index < sub_counts[0])]
where the time goes in v2:
time: 40.7 us; the launch traced here: 40.6 us
  Pallas kernels  39.9 us (98%)
  between operations  0.66 us (2%)
    pallas_call x1, Pallas kernels, coarse(): pl.pallas_call(coarse_kernel, out_shape=jax.ShapeDtypeStruct((16, LANES),...  36.4 us
    pallas_call x1, Pallas kernels, project(): pl.pallas_call(project_kernel, out_shape=jax.ShapeDtypeStruct(duals.shape...  3.5 us

profile of v2, /device:TPU:1, one launch (start us, length us, event | category | flops | bytes accessed | tf_op | source)
XLA Modules:
  0.0 40.6 jit_solution(5580549939903513000)
XLA Ops:
  0.7 36.4 %shard_map.73.corr = bf16[16,128]{1,0:T(8,128)(2,1)} custom-call(bf16[96,2,3840]{2,1,0:T(2,128)(2,1)} %duals.3, bf16[6,2,3840]{2,1,0:T(2,128)(2,1)} %bitcast.4, s32[1]{0:T(128)S(6)} %copy.8.counts, s32[2]{0:T(128)} %sizes.3, f32[96,96]{1,0:T(8,128)} %bitcast.6, s32[1,96]{1,0:T(1,128)} %cmap_in.1, f32[192,1536]{1,0:T(8,128)} %bitcast.3), custom_call_target="tpu_custom_call" | custom-call | tf_op jit(solution)/shard_map/pallas_call | solution.py:309
  37.1 3.5 %shard_map.74 = bf16[96,2,3840]{2,1,0:T(2,128)(2,1)} custom-call(bf16[96,2,3840]{2,1,0:T(2,128)(2,1)} %duals.3, bf16[6,2,3840]{2,1,0:T(2,128)(2,1)} %bitcast.5, s32[1]{0:T(128)S(6)} %copy.8.counts, s32[2]{0:T(128)} %sizes.3, bf16[16,128]{1,0:T(8,128)(2,1)} %shard_map.73.corr), custom_call_target="tpu_custom_call" | custom-call | tf_op jit(solution)/shard_map/pallas_call | solution.py:383

commit v3 on v2

--- a/solution.py
+++ b/solution.py
@@ -15,6 +15,7 @@
 CK = 96
 RHS = 96
 LANES = 128
+SPAN = CK + BAND
 
 
 def mm(a, b, dims=((1,), (0,))):
@@ -59,16 +60,15 @@
 
 
 def coarse_kernel(
-    duals, kern, counts, sizes, low_in, cmap_in, ct, out,
-    dbuf, kbuf, nbuf, sbuf, low, cmap,
-    ysend, yall, gsec, gprev, cst, cpk, c48, gbuf, part, crecv,
-    isem, lsem, y_s, y_r, g_s, g_r, c_s, c_r, z_s, z_r, v_s, v_r, d_s, d_r,
+    duals, kern, counts, sizes, low_in, cmap_in, ct, out, dbuf, mbuf,
+    kbuf, nbuf, sbuf, low, cmap,
+    ysend, yall, cst, cpk, c48, blocks, part, crecv,
+    isem, lsem, y_s, y_r, c_s, c_r, z_s, z_r, v_s, v_r, d_s, d_r,
 ):
     w = lax.axis_index("wide")
     t = lax.axis_index("clus")
     z, y = w // NY, w % NY
-    wn, wp = (w + 1) % NW, (w + NW - 1) % NW
-    root_n = (wn // NY) % NT
+    wn = (w + 1) % NW
     is_root = t == z % NT
     zh = z // NT
     cs0, cs1 = w // NT, wn // NT
@@ -79,7 +79,14 @@
     def zdev(zz):
         return (zz * NY + y, t)
 
-    gbuf[...] = jnp.zeros_like(gbuf)
+    loads = [
+        pltpu.make_async_copy(src, dst, isem.at[i])
+        for i, (src, dst) in enumerate(
+            ((kern, kbuf), (counts, nbuf), (sizes, sbuf), (duals, dbuf), (low_in, low), (cmap_in, cmap))
+        )
+    ]
+    for load in loads:
+        load.start()
 
     barrier = pltpu.get_barrier_semaphore()
 
@@ -96,20 +103,6 @@
     for k in range(1, NY):
         greet((z * NY + (y + k) % NY, t))
 
-    @pl.when(is_root)
-    def _():
-        for k in range(NT):
-            greet(at(wp, k))
-
-    loads = [
-        pltpu.make_async_copy(src, dst, isem.at[i])
-        for i, (src, dst) in enumerate(
-            ((kern, kbuf), (counts, nbuf), (sizes, sbuf), (duals, dbuf), (low_in, low), (cmap_in, cmap))
-        )
-    ]
-    for load in loads:
-        load.start()
-
     @pl.when(t == cs0)
     def _():
         pltpu.make_async_copy(
@@ -125,22 +118,20 @@
     ysend[...] = jnp.zeros_like(ysend)
     for load in loads[:4]:
         load.wait()
-    masked = masked_rows(kbuf[...], nbuf[0], sbuf[0], sbuf[1]).reshape(6, 2, -1)
+    masked = masked_rows(kbuf[...], nbuf[0], sbuf[0], sbuf[1])
+    mbuf[...] = masked
+    masked = masked.reshape(6, 2, -1)
     local = lax.dot_general(
         masked, dbuf[...], (((2,), (2,)), ((1,), (1,))), preferred_element_type=jnp.float32
     )
     for slot in range(2):
         ysend[pl.ds(slot, 6, stride=2), 0:RHS] = local[slot]
 
-    pl.semaphore_wait(barrier, jnp.where(is_root, 26, 11))
-
-    to_next = pltpu.make_async_remote_copy(
-        ysend, yall.at[NT + t], y_s.at[0], y_r.at[NT + t], at(wn, root_n), MESH
-    )
+    pl.semaphore_wait(barrier, jnp.where(is_root, 25, 10))
+
     to_own = pltpu.make_async_remote_copy(
-        ysend, yall.at[t], y_s.at[1], y_r.at[t], at(w, z % NT), MESH
-    )
-    to_next.start()
+        ysend, yall.at[t], y_s, y_r.at[t], at(w, z % NT), MESH
+    )
 
     @pl.when(jnp.logical_not(is_root))
     def _():
@@ -165,14 +156,17 @@
         def _():
             pltpu.make_async_copy(ct.at[pl.ds(0, BAND)], cst.at[half], lsem.at[half]).wait()
             for zz in range(NZ):
-                cpk[half, zz % NT, :, zz // NT * LANES : zz // NT * LANES + CK] = cst[
-                    half, :, zz * CK : zz * CK + CK
-                ]
-            for tt in range(NT):
-                for side in range(2):
-                    cpk[half, tt, :, side * LANES + CK : (side + 1) * LANES] = jnp.zeros(
-                        (BAND, LANES - CK), jnp.float32
-                    )
+                at_lane = zz // NT * LANES
+                if zz < NZ - 1:
+                    cpk[half, zz % NT, :, at_lane : at_lane + SPAN] = cst[
+                        half, :, zz * CK : zz * CK + SPAN
+                    ]
+                else:
+                    cpk[half, zz % NT, :, at_lane : at_lane + CK] = cst[half, :, zz * CK :]
+                    cpk[half, zz % NT, :, at_lane + CK : at_lane + SPAN] = cst[half, :, :BAND]
+                cpk[half, zz % NT, :, at_lane + SPAN : at_lane + LANES] = jnp.zeros(
+                    (BAND, LANES - SPAN), jnp.float32
+                )
             for k in range(1, NT):
                 cpiece(half, (t + k) % NT, k).start()
             c48[half] = cpk[half, t]
@@ -191,35 +185,29 @@
     rel = jnp.where(rel < 0, rel + GK, rel)
     pt = jnp.where(rel == lax.broadcasted_iota(jnp.int32, (2 * BAND, CK), 0), 1.0, 0.0)
     g = mm(pt, lpad)
-    gsec[...] = g[BAND:]
-
-    send_g = pltpu.make_async_remote_copy(gsec, gprev, g_s, g_r, at(wn, root_n), MESH)
-
-    @pl.when(t == root_n)
-    def _():
-        send_g.start()
 
     def zcopy(k):
-        rows = pl.ds(pl.multiple_of(y * BAND, 8), BAND)
-        return pltpu.make_async_remote_copy(
-            gbuf.at[zh, rows], gbuf.at[zh, rows], z_s.at[k], z_r.at[zh], zdev((z + k) % NZ), MESH
-        )
+        return pltpu.make_async_remote_copy(
+            blocks.at[zh, y], blocks.at[zh, y], z_s.at[k], z_r.at[zh], zdev((z + k) % NZ), MESH
+        )
+
+    @pl.when(jnp.logical_not(is_root))
+    def _():
+        part[...] = jnp.zeros_like(part)
 
     @pl.when(is_root)
     def _():
-        for k in range(2 * NT):
+        for k in range(NT):
             @pl.when(k != t)
             def _():
                 pltpu.make_async_remote_copy(
-                    ysend, yall.at[k], y_s.at[1], y_r.at[k], at(w, t), MESH
+                    ysend, yall.at[k], y_s, y_r.at[k], at(w, t), MESH
                 ).wait_recv()
-        send_g.wait_recv()
-        own = yall[0:NT].reshape(NT * 16, LANES)
-        prev = yall[NT : 2 * NT].reshape(NT * 16, LANES)
-        gs = mm(g[:BAND], own) + mm(gprev[...], prev)
-        gbuf[zh, pl.ds(pl.multiple_of(y * BAND, 8), BAND), :] = gs
+        own = yall[...].reshape(NT * 16, LANES)
+        blocks[zh, y] = mm(g, own)
         for k in (8, 7, 9, 6, 10, 5, 11, 4, 12, 3, 13, 2, 14, 1, 15):
             zcopy(k).start()
+        part[...] = mm(lpad, mm(lpad, own), ((0,), (0,))).reshape(NT, 16, LANES)
 
     for half, src in ((0, cs0), (1, cs1)):
         @pl.when(t != src)
@@ -229,23 +217,21 @@
     oper = mm(g, c2, ((0,), (0,)))
 
     def ycopy(h, k):
-        rows = pl.ds(pl.multiple_of(y * BAND, 8), BAND)
-        return pltpu.make_async_remote_copy(
-            gbuf.at[h, rows], gbuf.at[h, rows], v_s.at[h, k], v_r.at[h, k], (z * NY + (y + k) % NY, t), MESH
+        return pltpu.make_async_remote_copy(
+            blocks.at[h, y], blocks.at[h, y], v_s.at[h, k], v_r.at[h, k], (z * NY + (y + k) % NY, t), MESH
         )
 
     def yrecv(h, k):
-        rows = pl.ds(pl.multiple_of((y + NY - k) % NY * BAND, 8), BAND)
-        return pltpu.make_async_remote_copy(
-            gbuf.at[h, rows], gbuf.at[h, rows], v_s.at[h, k], v_r.at[h, k], (z * NY + (y + k) % NY, t), MESH
+        return pltpu.make_async_remote_copy(
+            blocks.at[h, y], blocks.at[h, (y + NY - k) % NY], v_s.at[h, k], v_r.at[h, k],
+            (z * NY + (y + k) % NY, t), MESH,
         )
 
     for h in range(2):
         @pl.when(jnp.logical_not(is_root & (zh == h)))
         def _():
-            rows = pl.ds(pl.multiple_of(y * BAND, 8), BAND)
             pltpu.make_async_remote_copy(
-                gbuf.at[h, rows], gbuf.at[h, rows], z_s.at[0], z_r.at[h], zdev((z + 1) % NZ), MESH
+                blocks.at[h, y], blocks.at[h, y], z_s.at[0], z_r.at[h], zdev((z + 1) % NZ), MESH
             ).wait_recv()
         for k in (2, 1, 3):
             ycopy(h, k).start()
@@ -253,13 +239,14 @@
         for k in range(1, NY):
             yrecv(h, k).wait_recv()
 
-    total = -mm(oper, gbuf[...].reshape(2 * LANES, LANES))
-    part[...] = total.reshape(NT, 16, LANES)
-
-    @pl.when(is_root)
-    def _():
-        own = yall[0:NT].reshape(NT * 16, LANES)
-        part[...] += mm(lpad, mm(lpad, own), ((0,), (0,))).reshape(NT, 16, LANES)
+    rows = []
+    for h in range(2):
+        rows.append(blocks[h, 0, :BAND])
+        for yy in range(1, NY):
+            rows.append(blocks[h, yy - 1, BAND:] + blocks[h, yy, :BAND])
+        rows.append(blocks[h, NY - 1, BAND:])
+        rows.append(jnp.zeros((LANES - SPAN, LANES), jnp.float32))
+    part[...] -= mm(oper, jnp.concatenate(rows, axis=0)).reshape(NT, 16, LANES)
 
     def dcopy(k):
         return pltpu.make_async_remote_copy(
@@ -274,8 +261,6 @@
         acc += crecv[k]
     out[...] = acc.astype(out.dtype)
 
-    to_next.wait_send()
-
     @pl.when(jnp.logical_not(is_root))
     def _():
         to_own.wait_send()
@@ -285,10 +270,6 @@
         def _():
             for k in range(1, NT):
                 cpiece(half, (t + k) % NT, k).wait_send()
-
-    @pl.when(t == root_n)
-    def _():
-        send_g.wait_send()
 
     @pl.when(is_root)
     def _():
@@ -308,30 +289,30 @@
     dma = pltpu.SemaphoreType.DMA
     return pl.pallas_call(
         coarse_kernel,
-        out_shape=jax.ShapeDtypeStruct((16, LANES), jnp.bfloat16),
+        out_shape=[
+            pltpu.VMEM((16, LANES), jnp.bfloat16),
+            pltpu.VMEM(duals.shape, duals.dtype),
+            pltpu.VMEM((12, duals.shape[2]), duals.dtype),
+        ],
         in_specs=[hbm] * 7,
-        out_specs=pl.BlockSpec(memory_space=pltpu.VMEM),
+        out_specs=[pl.BlockSpec(memory_space=pltpu.VMEM)] * 3,
         scratch_shapes=[
-            pltpu.VMEM(duals.shape, duals.dtype),
             pltpu.VMEM(kern.shape, kern.dtype),
             pltpu.SMEM(counts.shape, jnp.int32),
             pltpu.SMEM(sizes.shape, jnp.int32),
             pltpu.VMEM(low.shape, f32),
             pltpu.VMEM(cmap.shape, jnp.int32),
             pltpu.VMEM((16, LANES), f32),
-            pltpu.VMEM((2 * NT, 16, LANES), f32),
-            pltpu.VMEM((BAND, LANES), f32),
-            pltpu.VMEM((BAND, LANES), f32),
+            pltpu.VMEM((NT, 16, LANES), f32),
             pltpu.VMEM((2, BAND, GK), f32),
             pltpu.VMEM((2, NT, BAND, 2 * LANES), f32),
             pltpu.VMEM((2, BAND, 2 * LANES), f32),
-            pltpu.VMEM((2, LANES, LANES), f32),
+            pltpu.VMEM((2, NY, 2 * BAND, LANES), f32),
             pltpu.VMEM((NT, 16, LANES), f32),
             pltpu.VMEM((NT, 16, LANES), f32),
             dma((6,)),
             dma((2,)),
-            dma((2,)), dma((2 * NT,)),
-            dma, dma,
+            dma, dma((NT,)),
             dma((2, NT)), dma((2,)),
             dma((NZ,)), dma((2,)),
             dma((2, NY)), dma((2, NY)),
@@ -344,8 +325,8 @@
 PIECES = 6
 
 
-def project_kernel(duals, kern, counts, sizes, corr, out, obuf, sem):
-    masked = masked_rows(kern[...], counts[0], sizes[0], sizes[1])
+def project_kernel(duals, masked_in, corr, out, obuf, sem):
+    masked = masked_in[...]
     rows = 2 * RHS
     pick = jnp.where(
         lax.broadcasted_iota(jnp.int32, (rows, LANES), 0) // 2
@@ -377,27 +358,27 @@
         copy.wait()
 
 
-def project(duals, kern, counts, sizes, corr):
+def project(duals, masked, corr):
     vmem = pl.BlockSpec(memory_space=pltpu.VMEM)
-    smem = pl.BlockSpec(memory_space=pltpu.SMEM)
     return pl.pallas_call(
         project_kernel,
         out_shape=jax.ShapeDtypeStruct(duals.shape, duals.dtype),
-        in_specs=[vmem, vmem, smem, smem, vmem],
+        in_specs=[vmem, vmem, vmem],
         out_specs=pl.BlockSpec(memory_space=pl.ANY),
         scratch_shapes=[
             pltpu.VMEM(duals.shape, duals.dtype),
             pltpu.SemaphoreType.DMA((PIECES,)),
         ],
-    )(duals, kern, counts, sizes, corr)
+        compiler_params=pltpu.CompilerParams(vmem_limit_bytes=24 << 20),
+    )(duals, masked, corr)
 
 
 def per_device(duals, kernel, sub_counts, dual_sizes, cluster_factor, coarse_map, coarse_inverse):
     kern = kernel.transpose(1, 0, 2)
-    corr = coarse(
+    corr, held, masked = coarse(
         duals, kern, sub_counts, dual_sizes, cluster_factor[0], coarse_map, coarse_inverse.T
     )
-    return project(duals, kern, sub_counts, dual_sizes, corr)
+    return project(held, masked, corr)
 
 
 def solution(mesh):

time: 40.7 us -> 38.5 us (0.946)
  Pallas kernels: 39.9 us -> 37.7 us
    pallas_call x1, Pallas kernels: 3.5 us -> 2.07 us  [project(): pl.pallas_call(project_kernel, out_shape=jax.ShapeDtypeStruct(duals.shape...]
    pallas_call x1, Pallas kernels: 36.4 us -> 35.6 us  [coarse(): pl.pallas_call(coarse_kernel, out_shape=[pltpu.VMEM((16, LANES), jnp.bflo...]
where the time goes in v3:
time: 38.5 us; the launch traced here: 38.3 us
  Pallas kernels  37.7 us (98%)
  between operations  0.66 us (2%)
    pallas_call x1, Pallas kernels, coarse(): pl.pallas_call(coarse_kernel, out_shape=[pltpu.VMEM((16, LANES), jnp.bflo...  35.6 us
    pallas_call x1, Pallas kernels, project(): pl.pallas_call(project_kernel, out_shape=jax.ShapeDtypeStruct(duals.shape...  2.07 us

profile of v3, /device:TPU:1, one launch (start us, length us, event | category | flops | bytes accessed | tf_op | source)
XLA Modules:
  0.0 38.3 jit_solution(6778376340468868763)
XLA Ops:
  0.7 35.6 %shard_map.73 = (bf16[16,128]{1,0:T(8,128)(2,1)S(1)}, bf16[96,2,3840]{2,1,0:T(2,128)(2,1)S(1)}, bf16[12,3840]{1,0:T(8,128)(2,1)S(1)}) custom-call(bf16[96,2,3840]{2,1,0:T(2,128)(2,1)} %duals.1, bf16[6,2,3840]{2,1,0:T(2,128)(2,1)} %bitcast.4, s32[1]{0:T(128)S(6)} %copy.8.counts, s32[2]{0:T(128)} %sizes.1, f32[96,96]{1,0:T(8,128)} %bitcast.5, ...), custom_call_target="tpu_custom_call" | custom-call | tf_op jit(solution)/shard_map/pallas_call | solution.py:290
  36.2 2.1 %shard_map.74 = bf16[96,2,3840]{2,1,0:T(2,128)(2,1)} custom-call(bf16[96,2,3840]{2,1,0:T(2,128)(2,1)S(1)} %get-tuple-element.8.duals, bf16[12,3840]{1,0:T(8,128)(2,1)S(1)} %get-tuple-element.9.masked_in, bf16[16,128]{1,0:T(8,128)(2,1)S(1)} %get-tuple-element.10.corr), custom_call_target="tpu_custom_call" | custom-call | tf_op jit(solution)/shard_map/pallas_call | solution.py:363

commit v4 on v3

--- a/solution.py
+++ b/solution.py
@@ -51,6 +51,10 @@
     return x
 
 
+def root_place(z):
+    return 2 * (z % 4) + z // 4 % 2
+
+
 def masked_rows(kern, count, size0, size1):
     rows = kern.reshape(12, kern.shape[-1])
     slot = lax.broadcasted_iota(jnp.int32, rows.shape, 0) % 2
@@ -62,14 +66,16 @@
 def coarse_kernel(
     duals, kern, counts, sizes, low_in, cmap_in, ct, out, dbuf, mbuf,
     kbuf, nbuf, sbuf, low, cmap,
-    ysend, yall, cst, cpk, c48, blocks, part, crecv,
+    ysend, yall, lpad, gop, oper, cst, cpk, c48, blocks, part, crecv,
     isem, lsem, y_s, y_r, c_s, c_r, z_s, z_r, v_s, v_r, d_s, d_r,
 ):
     w = lax.axis_index("wide")
     t = lax.axis_index("clus")
     z, y = w // NY, w % NY
     wn = (w + 1) % NW
-    is_root = t == z % NT
+    root = root_place(z)
+    is_root = t == root
+    z0 = t // 2 + 4 * (t % 2)
     zh = z // NT
     cs0, cs1 = w // NT, wn // NT
 
@@ -93,7 +99,7 @@
     def greet(dev):
         pl.semaphore_signal(barrier, inc=1, device_id=dev, device_id_type=MESH)
 
-    for zz in (t, t + NT):
+    for zz in (z0, z0 + NT):
         @pl.when(zz != z)
         def _():
             greet(zdev(zz))
@@ -114,6 +120,26 @@
         pltpu.make_async_copy(
             ct.at[pl.ds(pl.multiple_of((wn % NT) * BAND, 8), BAND)], cst.at[1], lsem.at[1]
         ).start()
+
+    def operators():
+        for load in loads[4:]:
+            load.wait()
+        mi = lax.broadcasted_iota(jnp.int32, (CK, LANES), 0)
+        pi = lax.broadcasted_iota(jnp.int32, (CK, LANES), 1)
+        slot_row = pi % 16
+        spread = jnp.where(
+            (mi == 12 * (pi // 16) + 6 * (slot_row % 2) + slot_row // 2) & (slot_row < 12), 1.0, 0.0
+        )
+        linv = mm(lower_inverse(low[...]), spread)
+        lpad[...] = linv
+        rel = cmap[...] - w * BAND
+        rel = jnp.where(rel < 0, rel + GK, rel)
+        pt = jnp.where(rel == lax.broadcasted_iota(jnp.int32, (2 * BAND, CK), 0), 1.0, 0.0)
+        gop[...] = mm(pt, linv)
+
+    @pl.when(is_root)
+    def _():
+        operators()
 
     ysend[...] = jnp.zeros_like(ysend)
     for load in loads[:4]:
@@ -130,7 +156,7 @@
     pl.semaphore_wait(barrier, jnp.where(is_root, 25, 10))
 
     to_own = pltpu.make_async_remote_copy(
-        ysend, yall.at[t], y_s, y_r.at[t], at(w, z % NT), MESH
+        ysend, yall.at[t], y_s, y_r.at[t], at(w, root), MESH
     )
 
     @pl.when(jnp.logical_not(is_root))
@@ -157,34 +183,24 @@
             pltpu.make_async_copy(ct.at[pl.ds(0, BAND)], cst.at[half], lsem.at[half]).wait()
             for zz in range(NZ):
                 at_lane = zz // NT * LANES
+                tt = root_place(zz)
                 if zz < NZ - 1:
-                    cpk[half, zz % NT, :, at_lane : at_lane + SPAN] = cst[
+                    cpk[half, tt, :, at_lane : at_lane + SPAN] = cst[
                         half, :, zz * CK : zz * CK + SPAN
                     ]
                 else:
-                    cpk[half, zz % NT, :, at_lane : at_lane + CK] = cst[half, :, zz * CK :]
-                    cpk[half, zz % NT, :, at_lane + CK : at_lane + SPAN] = cst[half, :, :BAND]
-                cpk[half, zz % NT, :, at_lane + SPAN : at_lane + LANES] = jnp.zeros(
+                    cpk[half, tt, :, at_lane : at_lane + CK] = cst[half, :, zz * CK :]
+                    cpk[half, tt, :, at_lane + CK : at_lane + SPAN] = cst[half, :, :BAND]
+                cpk[half, tt, :, at_lane + SPAN : at_lane + LANES] = jnp.zeros(
                     (BAND, LANES - SPAN), jnp.float32
                 )
             for k in range(1, NT):
                 cpiece(half, (t + k) % NT, k).start()
             c48[half] = cpk[half, t]
 
-    for load in loads[4:]:
-        load.wait()
-    linv = lower_inverse(low[...])
-    mi = lax.broadcasted_iota(jnp.int32, (CK, LANES), 0)
-    pi = lax.broadcasted_iota(jnp.int32, (CK, LANES), 1)
-    slot_row = pi % 16
-    spread = jnp.where(
-        (mi == 12 * (pi // 16) + 6 * (slot_row % 2) + slot_row // 2) & (slot_row < 12), 1.0, 0.0
-    )
-    lpad = mm(linv, spread)
-    rel = cmap[...] - w * BAND
-    rel = jnp.where(rel < 0, rel + GK, rel)
-    pt = jnp.where(rel == lax.broadcasted_iota(jnp.int32, (2 * BAND, CK), 0), 1.0, 0.0)
-    g = mm(pt, lpad)
+    @pl.when(jnp.logical_not(is_root))
+    def _():
+        operators()
 
     def zcopy(k):
         return pltpu.make_async_remote_copy(
@@ -204,17 +220,19 @@
                     ysend, yall.at[k], y_s, y_r.at[k], at(w, t), MESH
                 ).wait_recv()
         own = yall[...].reshape(NT * 16, LANES)
-        blocks[zh, y] = mm(g, own)
+        blocks[zh, y] = mm(gop[...], own)
         for k in (8, 7, 9, 6, 10, 5, 11, 4, 12, 3, 13, 2, 14, 1, 15):
             zcopy(k).start()
-        part[...] = mm(lpad, mm(lpad, own), ((0,), (0,))).reshape(NT, 16, LANES)
+        part[...] = mm(lpad[...], mm(lpad[...], own), ((0,), (0,))).reshape(NT, 16, LANES)
 
     for half, src in ((0, cs0), (1, cs1)):
         @pl.when(t != src)
         def _():
             cpiece(half, t, 0).wait_recv()
     c2 = c48[...].reshape(2 * BAND, 2 * LANES)
-    oper = mm(g, c2, ((0,), (0,)))
+    both = mm(gop[...], c2, ((0,), (0,)))
+    for h in range(2):
+        oper[h] = both[:, h * LANES : (h + 1) * LANES]
 
     def ycopy(h, k):
         return pltpu.make_async_remote_copy(
@@ -227,7 +245,9 @@
             (z * NY + (y + k) % NY, t), MESH,
         )
 
-    for h in range(2):
+    away = (z + NZ - z0) % NZ
+    near = jnp.where(jnp.minimum(away, NZ - away) <= NZ // 4, 0, 1)
+    for h in (near, 1 - near):
         @pl.when(jnp.logical_not(is_root & (zh == h)))
         def _():
             pltpu.make_async_remote_copy(
@@ -235,18 +255,15 @@
             ).wait_recv()
         for k in (2, 1, 3):
             ycopy(h, k).start()
-    for h in range(2):
+    for h in (near, 1 - near):
         for k in range(1, NY):
             yrecv(h, k).wait_recv()
-
-    rows = []
-    for h in range(2):
-        rows.append(blocks[h, 0, :BAND])
+        rows = [blocks[h, 0, :BAND]]
         for yy in range(1, NY):
             rows.append(blocks[h, yy - 1, BAND:] + blocks[h, yy, :BAND])
         rows.append(blocks[h, NY - 1, BAND:])
         rows.append(jnp.zeros((LANES - SPAN, LANES), jnp.float32))
-    part[...] -= mm(oper, jnp.concatenate(rows, axis=0)).reshape(NT, 16, LANES)
+        part[...] -= mm(oper[h], jnp.concatenate(rows, axis=0)).reshape(NT, 16, LANES)
 
     def dcopy(k):
         return pltpu.make_async_remote_copy(
@@ -304,6 +321,9 @@
             pltpu.VMEM(cmap.shape, jnp.int32),
             pltpu.VMEM((16, LANES), f32),
             pltpu.VMEM((NT, 16, LANES), f32),
+            pltpu.VMEM((CK, LANES), f32),
+            pltpu.VMEM((2 * BAND, LANES), f32),
+            pltpu.VMEM((2, LANES, LANES), f32),
             pltpu.VMEM((2, BAND, GK), f32),
             pltpu.VMEM((2, NT, BAND, 2 * LANES), f32),
             pltpu.VMEM((2, BAND, 2 * LANES), f32),

time: 38.5 us -> 36.2 us (0.940)
  Pallas kernels: 37.7 us -> 35.4 us
    pallas_call x1, Pallas kernels: 35.6 us -> 33.3 us  [coarse(): pl.pallas_call(coarse_kernel, out_shape=[pltpu.VMEM((16, LANES), jnp.bflo...]
where the time goes in v4:
time: 36.2 us; the launch traced here: 36.1 us
  Pallas kernels  35.4 us (98%)
  between operations  0.66 us (2%)
    pallas_call x1, Pallas kernels, coarse(): pl.pallas_call(coarse_kernel, out_shape=[pltpu.VMEM((16, LANES), jnp.bflo...  33.3 us
    pallas_call x1, Pallas kernels, project(): pl.pallas_call(project_kernel, out_shape=jax.ShapeDtypeStruct(duals.shape...  2.07 us

profile of v4, /device:TPU:1, one launch (start us, length us, event | category | flops | bytes accessed | tf_op | source)
XLA Modules:
  0.0 36.1 jit_solution(6048122971208965846)
XLA Ops:
  0.7 33.3 %shard_map.73 = (bf16[16,128]{1,0:T(8,128)(2,1)S(1)}, bf16[96,2,3840]{2,1,0:T(2,128)(2,1)S(1)}, bf16[12,3840]{1,0:T(8,128)(2,1)S(1)}) custom-call(bf16[96,2,3840]{2,1,0:T(2,128)(2,1)} %duals.1, bf16[6,2,3840]{2,1,0:T(2,128)(2,1)} %bitcast.4, s32[1]{0:T(128)S(6)} %copy.8.counts, s32[2]{0:T(128)} %sizes.1, f32[96,96]{1,0:T(8,128)} %bitcast.5, ...), custom_call_target="tpu_custom_call" | custom-call | tf_op jit(solution)/shard_map/pallas_call | solution.py:307
  34.0 2.1 %shard_map.74 = bf16[96,2,3840]{2,1,0:T(2,128)(2,1)} custom-call(bf16[96,2,3840]{2,1,0:T(2,128)(2,1)S(1)} %get-tuple-element.8.duals, bf16[12,3840]{1,0:T(8,128)(2,1)S(1)} %get-tuple-element.9.masked_in, bf16[16,128]{1,0:T(8,128)(2,1)S(1)} %get-tuple-element.10.corr), custom_call_target="tpu_custom_call" | custom-call | tf_op jit(solution)/shard_map/pallas_call | solution.py:383

commit v5 on v4

--- a/solution.py
+++ b/solution.py
@@ -52,7 +52,13 @@
 
 
 def root_place(z):
-    return 2 * (z % 4) + z // 4 % 2
+    x = z % 4
+    return 2 * x + (z // 4 + 1 + (x + 1) // 2) % 2
+
+
+def first_plane(t):
+    x = t // 2
+    return x + 4 * ((t + 1 + (x + 1) // 2) % 2)
 
 
 def masked_rows(kern, count, size0, size1):
@@ -75,7 +81,7 @@
     wn = (w + 1) % NW
     root = root_place(z)
     is_root = t == root
-    z0 = t // 2 + 4 * (t % 2)
+    z0 = first_plane(t)
     zh = z // NT
     cs0, cs1 = w // NT, wn // NT
 
@@ -84,15 +90,6 @@
 
     def zdev(zz):
         return (zz * NY + y, t)
-
-    loads = [
-        pltpu.make_async_copy(src, dst, isem.at[i])
-        for i, (src, dst) in enumerate(
-            ((kern, kbuf), (counts, nbuf), (sizes, sbuf), (duals, dbuf), (low_in, low), (cmap_in, cmap))
-        )
-    ]
-    for load in loads:
-        load.start()
 
     barrier = pltpu.get_barrier_semaphore()
 
@@ -103,6 +100,15 @@
         @pl.when(zz != z)
         def _():
             greet(zdev(zz))
+
+    loads = [
+        pltpu.make_async_copy(src, dst, isem.at[i])
+        for i, (src, dst) in enumerate(
+            ((duals, dbuf), (kern, kbuf), (counts, nbuf), (sizes, sbuf), (low_in, low), (cmap_in, cmap))
+        )
+    ]
+    for load in loads:
+        load.start()
 
     for k in range(1, NT):
         greet(at(w, (t + k) % NT))
@@ -202,9 +208,20 @@
     def _():
         operators()
 
-    def zcopy(k):
+    def ycopy(h, k):
         return pltpu.make_async_remote_copy(
-            blocks.at[zh, y], blocks.at[zh, y], z_s.at[k], z_r.at[zh], zdev((z + k) % NZ), MESH
+            blocks.at[h, y], blocks.at[h, y], v_s.at[h, k], v_r.at[h, k], (z * NY + (y + k) % NY, t), MESH
+        )
+
+    def yrecv(h, k):
+        return pltpu.make_async_remote_copy(
+            blocks.at[h, y], blocks.at[h, (y + NY - k) % NY], v_s.at[h, k], v_r.at[h, k],
+            (z * NY + (y + k) % NY, t), MESH,
+        )
+
+    def zcopy(zz):
+        return pltpu.make_async_remote_copy(
+            blocks.at[zh, y], blocks.at[zh, y], z_s.at[zz], z_r.at[zh], zdev(zz), MESH
         )
 
     @pl.when(jnp.logical_not(is_root))
@@ -221,9 +238,26 @@
                 ).wait_recv()
         own = yall[...].reshape(NT * 16, LANES)
         blocks[zh, y] = mm(gop[...], own)
-        for k in (8, 7, 9, 6, 10, 5, 11, 4, 12, 3, 13, 2, 14, 1, 15):
-            zcopy(k).start()
+        for k in (2, 1, 3):
+            ycopy(zh, k).start()
+        for zz in (0, 1, 2, 3, 4, 5, 6, 7, 15, 14, 13, 12, 11, 10, 9, 8):
+            @pl.when(zz != z)
+            def _():
+                zcopy(zz).start()
         part[...] = mm(lpad[...], mm(lpad[...], own), ((0,), (0,))).reshape(NT, 16, LANES)
+
+    away = (z + NZ - z0) % NZ
+    near = jnp.where(jnp.minimum(away, NZ - away) <= NZ // 4, 0, 1)
+    def forward(h):
+        @pl.when(jnp.logical_not(is_root & (zh == h)))
+        def _():
+            pltpu.make_async_remote_copy(
+                blocks.at[h, y], blocks.at[h, y], z_s.at[0], z_r.at[h], zdev((z + 1) % NZ), MESH
+            ).wait_recv()
+            for k in (2, 1, 3):
+                ycopy(h, k).start()
+
+    forward(near)
 
     for half, src in ((0, cs0), (1, cs1)):
         @pl.when(t != src)
@@ -234,27 +268,8 @@
     for h in range(2):
         oper[h] = both[:, h * LANES : (h + 1) * LANES]
 
-    def ycopy(h, k):
-        return pltpu.make_async_remote_copy(
-            blocks.at[h, y], blocks.at[h, y], v_s.at[h, k], v_r.at[h, k], (z * NY + (y + k) % NY, t), MESH
-        )
-
-    def yrecv(h, k):
-        return pltpu.make_async_remote_copy(
-            blocks.at[h, y], blocks.at[h, (y + NY - k) % NY], v_s.at[h, k], v_r.at[h, k],
-            (z * NY + (y + k) % NY, t), MESH,
-        )
-
-    away = (z + NZ - z0) % NZ
-    near = jnp.where(jnp.minimum(away, NZ - away) <= NZ // 4, 0, 1)
-    for h in (near, 1 - near):
-        @pl.when(jnp.logical_not(is_root & (zh == h)))
-        def _():
-            pltpu.make_async_remote_copy(
-                blocks.at[h, y], blocks.at[h, y], z_s.at[0], z_r.at[h], zdev((z + 1) % NZ), MESH
-            ).wait_recv()
-        for k in (2, 1, 3):
-            ycopy(h, k).start()
+    forward(1 - near)
+
     for h in (near, 1 - near):
         for k in range(1, NY):
             yrecv(h, k).wait_recv()
@@ -267,17 +282,11 @@
 
     def dcopy(k):
         return pltpu.make_async_remote_copy(
-            part.at[(t + k) % NT], crecv.at[k], d_s.at[k], d_r.at[k], at(w, (t + k) % NT), MESH
+            part.at[(t + k) % NT], crecv.at[k], d_s, d_r, at(w, (t + k) % NT), MESH
         )
 
     for k in (4, 3, 5, 2, 6, 1, 7):
         dcopy(k).start()
-    acc = part[t]
-    for k in range(1, NT):
-        dcopy(k).wait_recv()
-        acc += crecv[k]
-    out[...] = acc.astype(out.dtype)
-
     @pl.when(jnp.logical_not(is_root))
     def _():
         to_own.wait_send()
@@ -290,14 +299,23 @@
 
     @pl.when(is_root)
     def _():
-        for k in range(1, NZ):
-            zcopy(k).wait_send()
+        for zz in range(NZ):
+            @pl.when(zz != z)
+            def _():
+                zcopy(zz).wait_send()
 
     for h in range(2):
         for k in range(1, NY):
             ycopy(h, k).wait_send()
-    for k in range(1, NT):
-        dcopy(k).wait_send()
+    others = pl.ds(1, NT - 1)
+    pieces = pltpu.make_async_remote_copy(
+        crecv.at[others], crecv.at[others], d_s, d_r, at(w, (t + 1) % NT), MESH
+    )
+    pieces.wait_recv()
+    acc = part[t] + jnp.sum(crecv[1:], axis=0)
+    out[...] = acc.astype(out.dtype)
+
+    pieces.wait_send()
 
 
 def coarse(duals, kern, counts, sizes, low, cmap, ct):
@@ -336,7 +354,7 @@
             dma((2, NT)), dma((2,)),
             dma((NZ,)), dma((2,)),
             dma((2, NY)), dma((2, NY)),
-            dma((NT,)), dma((NT,)),
+            dma, dma,
         ],
         compiler_params=pltpu.CompilerParams(collective_id=0, has_side_effects=True),
     )(duals, kern, counts, sizes, low, cmap, ct)

time: 36.2 us -> 35.5 us (0.981)
  Pallas kernels: 35.4 us -> 34.6 us
    pallas_call x1, Pallas kernels: 33.3 us -> 32.6 us  [coarse(): pl.pallas_call(coarse_kernel, out_shape=[pltpu.VMEM((16, LANES), jnp.bflo...]
where the time goes in v5:
time: 35.5 us; the launch traced here: 35.3 us
  Pallas kernels  34.6 us (97%)
  between operations  0.66 us (2%)
    pallas_call x1, Pallas kernels, coarse(): pl.pallas_call(coarse_kernel, out_shape=[pltpu.VMEM((16, LANES), jnp.bflo...  32.6 us
    pallas_call x1, Pallas kernels, project(): pl.pallas_call(project_kernel, out_shape=jax.ShapeDtypeStruct(duals.shape...  2.07 us

profile of v5, /device:TPU:1, one launch (start us, length us, event | category | flops | bytes accessed | tf_op | source)
XLA Modules:
  0.0 35.3 jit_solution(13133933980836166177)
XLA Ops:
  0.7 32.6 %shard_map.73 = (bf16[16,128]{1,0:T(8,128)(2,1)S(1)}, bf16[96,2,3840]{2,1,0:T(2,128)(2,1)S(1)}, bf16[12,3840]{1,0:T(8,128)(2,1)S(1)}) custom-call(bf16[96,2,3840]{2,1,0:T(2,128)(2,1)} %duals.1, bf16[6,2,3840]{2,1,0:T(2,128)(2,1)} %bitcast.4, s32[1]{0:T(128)S(6)} %copy.8.counts, s32[2]{0:T(128)} %sizes.1, f32[96,96]{1,0:T(8,128)} %bitcast.5, ...), custom_call_target="tpu_custom_call" | custom-call | tf_op jit(solution)/shard_map/pallas_call | solution.py:325
  33.2 2.1 %shard_map.74 = bf16[96,2,3840]{2,1,0:T(2,128)(2,1)} custom-call(bf16[96,2,3840]{2,1,0:T(2,128)(2,1)S(1)} %get-tuple-element.8.duals, bf16[12,3840]{1,0:T(8,128)(2,1)S(1)} %get-tuple-element.9.masked_in, bf16[16,128]{1,0:T(8,128)(2,1)S(1)} %get-tuple-element.10.corr), custom_call_target="tpu_custom_call" | custom-call | tf_op jit(solution)/shard_map/pallas_call | solution.py:401

commit v6 on v5

--- a/solution.py
+++ b/solution.py
@@ -16,6 +16,7 @@
 RHS = 96
 LANES = 128
 SPAN = CK + BAND
+CHUNKS = 3
 
 
 def mm(a, b, dims=((1,), (0,))):
@@ -73,7 +74,7 @@
     duals, kern, counts, sizes, low_in, cmap_in, ct, out, dbuf, mbuf,
     kbuf, nbuf, sbuf, low, cmap,
     ysend, yall, lpad, gop, oper, cst, cpk, c48, blocks, part, crecv,
-    isem, lsem, y_s, y_r, c_s, c_r, z_s, z_r, v_s, v_r, d_s, d_r,
+    isem, dsem, lsem, y_s, y_r, c_s, c_r, z_s, z_r, v_s, v_r, d_s, d_r,
 ):
     w = lax.axis_index("wide")
     t = lax.axis_index("clus")
@@ -104,10 +105,17 @@
     loads = [
         pltpu.make_async_copy(src, dst, isem.at[i])
         for i, (src, dst) in enumerate(
-            ((duals, dbuf), (kern, kbuf), (counts, nbuf), (sizes, sbuf), (low_in, low), (cmap_in, cmap))
+            ((kern, kbuf), (counts, nbuf), (sizes, sbuf), (low_in, low), (cmap_in, cmap))
         )
     ]
-    for load in loads:
+    width = duals.shape[2] // CHUNKS
+    chunks = [
+        pltpu.make_async_copy(
+            duals.at[:, :, pl.ds(i * width, width)], dbuf.at[:, :, pl.ds(i * width, width)], dsem.at[i]
+        )
+        for i in range(CHUNKS)
+    ]
+    for load in loads[:3] + chunks + loads[3:]:
         load.start()
 
     for k in range(1, NT):
@@ -128,7 +136,7 @@
         ).start()
 
     def operators():
-        for load in loads[4:]:
+        for load in loads[3:]:
             load.wait()
         mi = lax.broadcasted_iota(jnp.int32, (CK, LANES), 0)
         pi = lax.broadcasted_iota(jnp.int32, (CK, LANES), 1)
@@ -148,21 +156,28 @@
         operators()
 
     ysend[...] = jnp.zeros_like(ysend)
-    for load in loads[:4]:
+    for load in loads[:3]:
         load.wait()
     masked = masked_rows(kbuf[...], nbuf[0], sbuf[0], sbuf[1])
     mbuf[...] = masked
     masked = masked.reshape(6, 2, -1)
-    local = lax.dot_general(
-        masked, dbuf[...], (((2,), (2,)), ((1,), (1,))), preferred_element_type=jnp.float32
-    )
+    local = jnp.zeros((2, 6, RHS), jnp.float32)
+    for i, chunk in enumerate(chunks):
+        chunk.wait()
+        cols = slice(i * width, (i + 1) * width)
+        local += lax.dot_general(
+            masked[:, :, cols],
+            dbuf[:, :, cols],
+            (((2,), (2,)), ((1,), (1,))),
+            preferred_element_type=jnp.float32,
+        )
     for slot in range(2):
         ysend[pl.ds(slot, 6, stride=2), 0:RHS] = local[slot]
 
     pl.semaphore_wait(barrier, jnp.where(is_root, 25, 10))
 
     to_own = pltpu.make_async_remote_copy(
-        ysend, yall.at[t], y_s, y_r.at[t], at(w, root), MESH
+        ysend, yall.at[t], y_s, y_r, at(w, root), MESH
     )
 
     @pl.when(jnp.logical_not(is_root))
@@ -219,6 +234,12 @@
             (z * NY + (y + k) % NY, t), MESH,
         )
 
+    def ystart(h):
+        for yy in range(NY):
+            @pl.when(yy != y)
+            def _():
+                ycopy(h, (yy + NY - y) % NY).start()
+
     def zcopy(zz):
         return pltpu.make_async_remote_copy(
             blocks.at[zh, y], blocks.at[zh, y], z_s.at[zz], z_r.at[zh], zdev(zz), MESH
@@ -230,20 +251,20 @@
 
     @pl.when(is_root)
     def _():
-        for k in range(NT):
-            @pl.when(k != t)
-            def _():
-                pltpu.make_async_remote_copy(
-                    ysend, yall.at[k], y_s, y_r.at[k], at(w, t), MESH
-                ).wait_recv()
+        pltpu.make_async_remote_copy(
+            yall.at[pl.ds(0, NT - 1)], yall.at[pl.ds(0, NT - 1)], y_s, y_r, at(w, t), MESH
+        ).wait_recv()
         own = yall[...].reshape(NT * 16, LANES)
         blocks[zh, y] = mm(gop[...], own)
-        for k in (2, 1, 3):
-            ycopy(zh, k).start()
-        for zz in (0, 1, 2, 3, 4, 5, 6, 7, 15, 14, 13, 12, 11, 10, 9, 8):
-            @pl.when(zz != z)
-            def _():
-                zcopy(zz).start()
+        def zstart(planes):
+            for zz in planes:
+                @pl.when(zz != z)
+                def _():
+                    zcopy(zz).start()
+
+        zstart((0, 1, 2, 3))
+        ystart(zh)
+        zstart((4, 5, 6, 7, 15, 14, 13, 12, 11, 10, 9, 8))
         part[...] = mm(lpad[...], mm(lpad[...], own), ((0,), (0,))).reshape(NT, 16, LANES)
 
     away = (z + NZ - z0) % NZ
@@ -254,8 +275,7 @@
             pltpu.make_async_remote_copy(
                 blocks.at[h, y], blocks.at[h, y], z_s.at[0], z_r.at[h], zdev((z + 1) % NZ), MESH
             ).wait_recv()
-            for k in (2, 1, 3):
-                ycopy(h, k).start()
+            ystart(h)
 
     forward(near)
 
@@ -285,8 +305,11 @@
             part.at[(t + k) % NT], crecv.at[k], d_s, d_r, at(w, (t + k) % NT), MESH
         )
 
-    for k in (4, 3, 5, 2, 6, 1, 7):
-        dcopy(k).start()
+    for tt in (1, 3, 2, 5, 4, 7, 6, 0):
+        @pl.when(tt != t)
+        def _():
+            dcopy((tt + NT - t) % NT).start()
+
     @pl.when(jnp.logical_not(is_root))
     def _():
         to_own.wait_send()
@@ -348,9 +371,10 @@
             pltpu.VMEM((2, NY, 2 * BAND, LANES), f32),
             pltpu.VMEM((NT, 16, LANES), f32),
             pltpu.VMEM((NT, 16, LANES), f32),
-            dma((6,)),
+            dma((5,)),
+            dma((CHUNKS,)),
             dma((2,)),
-            dma, dma((NT,)),
+            dma, dma,
             dma((2, NT)), dma((2,)),
             dma((NZ,)), dma((2,)),
             dma((2, NY)), dma((2, NY)),

time: 35.5 us -> 35.1 us (0.989)
  no operation moved by 1% of the time
where the time goes in v6:
time: 35.1 us; the launch traced here: 35 us
  Pallas kernels  34.3 us (98%)
  between operations  0.66 us (2%)
    pallas_call x1, Pallas kernels, coarse(): pl.pallas_call(coarse_kernel, out_shape=[pltpu.VMEM((16, LANES), jnp.bflo...  32.3 us
    pallas_call x1, Pallas kernels, project(): pl.pallas_call(project_kernel, out_shape=jax.ShapeDtypeStruct(duals.shape...  2.07 us

profile of v6, /device:TPU:1, one launch (start us, length us, event | category | flops | bytes accessed | tf_op | source)
XLA Modules:
  0.0 35.0 jit_solution(10277405324699099949)
XLA Ops:
  0.7 32.3 %shard_map.73 = (bf16[16,128]{1,0:T(8,128)(2,1)S(1)}, bf16[96,2,3840]{2,1,0:T(2,128)(2,1)S(1)}, bf16[12,3840]{1,0:T(8,128)(2,1)S(1)}) custom-call(bf16[96,2,3840]{2,1,0:T(2,128)(2,1)} %duals.1, bf16[6,2,3840]{2,1,0:T(2,128)(2,1)} %bitcast.4, s32[1]{0:T(128)S(6)} %copy.8.counts, s32[2]{0:T(128)} %sizes.1, f32[96,96]{1,0:T(8,128)} %bitcast.5, ...), custom_call_target="tpu_custom_call" | custom-call | tf_op jit(solution)/shard_map/pallas_call | solution.py:348
  32.9 2.1 %shard_map.74 = bf16[96,2,3840]{2,1,0:T(2,128)(2,1)} custom-call(bf16[96,2,3840]{2,1,0:T(2,128)(2,1)S(1)} %get-tuple-element.8.duals, bf16[12,3840]{1,0:T(8,128)(2,1)S(1)} %get-tuple-element.9.masked_in, bf16[16,128]{1,0:T(8,128)(2,1)S(1)} %get-tuple-element.10.corr), custom_call_target="tpu_custom_call" | custom-call | tf_op jit(solution)/shard_map/pallas_call | solution.py:425

commit v7 on v6

--- a/solution.py
+++ b/solution.py
@@ -23,6 +23,16 @@
     return lax.dot_general(
         a, b, (dims, ((), ())), precision=lax.Precision.HIGHEST, preferred_element_type=jnp.float32
     )
+
+
+def mm_split(a, b):
+    a_hi = a.astype(jnp.bfloat16)
+    a_lo = (a - a_hi.astype(jnp.float32)).astype(jnp.bfloat16)
+    b_hi = b.astype(jnp.bfloat16)
+    b_lo = (b - b_hi.astype(jnp.float32)).astype(jnp.bfloat16)
+    left = jnp.concatenate([a_hi, a_lo, a_hi], axis=1)
+    right = jnp.concatenate([b_hi, b_hi, b_lo], axis=0)
+    return jnp.dot(left, right, preferred_element_type=jnp.float32)
 
 
 def lower_inverse(lower):
@@ -255,7 +265,7 @@
             yall.at[pl.ds(0, NT - 1)], yall.at[pl.ds(0, NT - 1)], y_s, y_r, at(w, t), MESH
         ).wait_recv()
         own = yall[...].reshape(NT * 16, LANES)
-        blocks[zh, y] = mm(gop[...], own)
+        blocks[zh, y] = mm_split(gop[...], own)
         def zstart(planes):
             for zz in planes:
                 @pl.when(zz != z)
@@ -298,7 +308,7 @@
             rows.append(blocks[h, yy - 1, BAND:] + blocks[h, yy, :BAND])
         rows.append(blocks[h, NY - 1, BAND:])
         rows.append(jnp.zeros((LANES - SPAN, LANES), jnp.float32))
-        part[...] -= mm(oper[h], jnp.concatenate(rows, axis=0)).reshape(NT, 16, LANES)
+        part[...] -= mm_split(oper[h], jnp.concatenate(rows, axis=0)).reshape(NT, 16, LANES)
 
     def dcopy(k):
         return pltpu.make_async_remote_copy(

time: 35.1 us -> 35 us (level)
  no operation moved by 1% of the time
where the time goes in v7:
time: 35 us; the launch traced here: 34.9 us
  Pallas kernels  34.2 us (98%)
  between operations  0.66 us (2%)
    pallas_call x1, Pallas kernels, coarse(): pl.pallas_call(coarse_kernel, out_shape=[pltpu.VMEM((16, LANES), jnp.bflo...  32.2 us
    pallas_call x1, Pallas kernels, project(): pl.pallas_call(project_kernel, out_shape=jax.ShapeDtypeStruct(duals.shape...  2.07 us

profile of v7, /device:TPU:1, one launch (start us, length us, event | category | flops | bytes accessed | tf_op | source)
XLA Modules:
  0.0 34.9 jit_solution(2730190979265117872)
XLA Ops:
  0.7 32.2 %shard_map.73 = (bf16[16,128]{1,0:T(8,128)(2,1)S(1)}, bf16[96,2,3840]{2,1,0:T(2,128)(2,1)S(1)}, bf16[12,3840]{1,0:T(8,128)(2,1)S(1)}) custom-call(bf16[96,2,3840]{2,1,0:T(2,128)(2,1)} %duals.1, bf16[6,2,3840]{2,1,0:T(2,128)(2,1)} %bitcast.4, s32[1]{0:T(128)S(6)} %copy.8.counts, s32[2]{0:T(128)} %sizes.1, f32[96,96]{1,0:T(8,128)} %bitcast.5, ...), custom_call_target="tpu_custom_call" | custom-call | tf_op jit(solution)/shard_map/pallas_call | solution.py:358
  32.8 2.1 %shard_map.74 = bf16[96,2,3840]{2,1,0:T(2,128)(2,1)} custom-call(bf16[96,2,3840]{2,1,0:T(2,128)(2,1)S(1)} %get-tuple-element.8.duals, bf16[12,3840]{1,0:T(8,128)(2,1)S(1)} %get-tuple-element.9.masked_in, bf16[16,128]{1,0:T(8,128)(2,1)S(1)} %get-tuple-element.10.corr), custom_call_target="tpu_custom_call" | custom-call | tf_op jit(solution)/shard_map/pallas_call | solution.py:435
